TPU v7x, 32 devices: a whole 2x2x4 slice. The times are simulated.
32 devices in a mesh: imp: 8 (over z, x), adv: 4 (over y, core).
Axes of the slice: x: 2, y: 2, z: 4, core: 2. Of those that a mesh axis runs over, the one named last changes fastest.
Arguments:
- impression_vectors: bfloat16 [64, 16384], P(None, 'imp'), may hold values from -6 to 6
- advertiser_vectors: bfloat16 [64, 4096], P(None, ('imp', 'adv')), may hold values from -0.75 to 0.75
- spend_limits: float32 [4096], P(('imp', 'adv')), may hold values from 1024 to 8192
- capacity: float32 [16384], P('imp'), may hold values from 256 to 2048
- blocks: int32 [128, 4, 8], P('imp', 'adv'), may hold values from 0 to 31, as said below
- counts: int32 [128, 4], P('imp', 'adv'), may hold values from 1 to 8, as said below
Outputs:
- prices: float32 [4096], P(('imp', 'adv'))
- impression_duals: float32 [16384], P('imp')
- impression_grad: bfloat16 [64, 16384], P(None, ('imp', 'adv'))
- advertiser_grad: bfloat16 [64, 4096], P(None, ('imp', 'adv'))
Inputs may be any that keep to these rules, and one draw needn't show every extreme that they name: Block numbers. Entry [g, a, k] names a block b with (b) % (the size of adv) == a. The 8 entries of one list are distinct; entries at slots k >= counts[g, a] are padding and name valid blocks too. `counts`: every group has one index of adv whose count is 8.
All inputs are finite; a program needn't handle non-finite values.
Results may differ from a plain program's by a relative error of at most 0.012.
Values may be sent and summed in bfloat16 or wider, within the bound.
A program may use at most 64 MiB of HBM per device.

v0:
```python
import jax
import jax.numpy as jnp
from jax import lax
from jax.sharding import PartitionSpec as P

GROUP = 128
BLOCK = 128
ITERS = 3
BLK_DEV = 1


def local(impression_vectors, advertiser_vectors, spend_limits, capacity, blocks, counts):
    features = impression_vectors.shape[0]
    groups_here = blocks.shape[0]
    slot_count = blocks.shape[2]
    adv_devices = lax.axis_size("adv")
    block_ids = blocks.reshape(groups_here, slot_count)
    local_ids = block_ids // BLK_DEV // adv_devices * BLK_DEV + block_ids % BLK_DEV
    live_slots = (jnp.arange(slot_count)[None, :] < counts).astype(jnp.float32)
    viewers = impression_vectors.reshape(features, groups_here, GROUP)
    extent = slot_count * BLOCK
    own_count = spend_limits.shape[0]
    fetched = lax.all_gather(advertiser_vectors, "imp", axis=1, tiled=True)
    catalog = fetched.reshape(features, fetched.shape[1] // BLOCK, BLOCK)
    local_blocks = catalog.shape[1]

    def allocate(source, prices, duals, group_no):
        chosen = lax.dynamic_index_in_dim(local_ids, group_no, 0, keepdims=False)
        columns = jnp.take(source, chosen, axis=1).reshape(features, extent)
        viewer = lax.dynamic_index_in_dim(viewers, group_no, 1, keepdims=False)
        scores = lax.dot_general(
            viewer, columns, (((0,), (0,)), ((), ())), preferred_element_type=jnp.float32
        )
        charged = jnp.take(prices, chosen, axis=0).reshape(extent)
        shadow = lax.dynamic_slice_in_dim(duals, group_no * GROUP, GROUP)
        eligible = jnp.repeat(
            lax.dynamic_index_in_dim(live_slots, group_no, 0, keepdims=False), BLOCK
        )
        shares = jnp.clip(scores - charged[None, :] - shadow[:, None], 0.0, 1.0) * eligible[None, :]
        return (shares, chosen, columns, viewer)

    duals = jnp.zeros((groups_here * GROUP,), jnp.float32)
    range_prices = jnp.zeros((local_blocks, BLOCK), jnp.float32)
    range_limits = lax.all_gather(spend_limits, "imp", axis=0, tiled=True).reshape(
        local_blocks, BLOCK
    )
    for iteration in range(ITERS):
        totals_prices = range_prices

        def advance(group_no, pair):
            outlay, demand = pair
            shares, chosen, _, _ = allocate(catalog, totals_prices, duals, group_no)
            outlay = outlay.at[chosen].add(jnp.sum(shares, axis=0).reshape(slot_count, BLOCK))
            demand = lax.dynamic_update_slice_in_dim(
                demand, jnp.sum(shares, axis=1), group_no * GROUP, 0
            )
            return (outlay, demand)

        totals_start = (
            jnp.zeros((local_blocks, BLOCK), jnp.float32),
            jnp.zeros((groups_here * GROUP,), jnp.float32),
        )
        outlay, demand = lax.fori_loop(0, groups_here, advance, totals_start)
        outlay = lax.psum(outlay, "imp")
        dual_demand = demand
        dual_demand = lax.psum(dual_demand, "adv")
        duals = jnp.maximum(duals + dual_demand / capacity - 1.0, 0.0)
        range_prices = jnp.maximum(range_prices + outlay / range_limits - 1.0, 0.0)
    own_prices = lax.dynamic_slice_in_dim(
        range_prices.reshape(-1), lax.axis_index("imp") * own_count, own_count
    )

    def grad_step(group_no, pair):
        imp_part, adv_part = pair
        shares, chosen, columns, viewer = allocate(catalog, range_prices, duals, group_no)
        weights = shares.astype(jnp.bfloat16)
        imp_cols = lax.dot_general(
            columns, weights, (((1,), (1,)), ((), ())), preferred_element_type=jnp.float32
        )
        imp_part = lax.dynamic_update_slice_in_dim(imp_part, imp_cols, group_no * GROUP, 1)
        adv_terms = jnp.dot(viewer, weights, preferred_element_type=jnp.float32).reshape(
            features, slot_count, BLOCK
        )
        adv_part = adv_part.at[:, chosen].add(adv_terms)
        return (imp_part, adv_part)

    start = (
        jnp.zeros((features, groups_here * GROUP), jnp.float32),
        jnp.zeros((features, local_blocks, BLOCK), jnp.float32),
    )
    imp_part, adv_part = lax.fori_loop(0, groups_here, grad_step, start)
    impression_grad = lax.psum_scatter(imp_part, "adv", scatter_dimension=1, tiled=True).astype(
        jnp.bfloat16
    )
    adv_rounded = (adv_part.reshape(features, -1) / GROUP).astype(jnp.bfloat16)
    advertiser_grad = (
        lax.psum_scatter(adv_rounded, "imp", scatter_dimension=1, tiled=True)
        .astype(jnp.float32)
        .astype(jnp.bfloat16)
    )
    return (own_prices, duals, impression_grad, advertiser_grad)


def solution(mesh):
    return jax.shard_map(
        local,
        mesh=mesh,
        in_specs=(
            P(None, "imp"),
            P(None, ("imp", "adv")),
            P(("imp", "adv")),
            P("imp"),
            P("imp", "adv", None),
            P("imp", "adv"),
        ),
        out_specs=(P(("imp", "adv")), P("imp"), P(None, ("imp", "adv")), P(None, ("imp", "adv"))),
        check_vma=False,
    )
```

profile of v0, /device:TPU:0, one launch (start us, length us, event | category | flops | bytes accessed | tf_op | source)
XLA Modules:
  0.0 400.0 jit_solution(3334277157712932147)
XLA Ops:
  7.2 0.9 copy-done
  8.8 27.9 %all_gather.6 = bf16[64,1024]{1,0:T(8,128)(2,1)S(1)} all-gather(bf16[64,128]{1,0:T(8,128)(2,1)S(1)} %copy-done.3), channel_id=1, replica_groups=mesh['imp'=8,'adv'=4] {'imp'}, dimensions={1}, use_global_device_ids=true | all-gather | bytes 147456 | tf_op jit(solution)/shard_map/all_gather | solution.py:23
  38.2 41.0 %while.60 = (s32[]{:T(128)}, f32[8,128]{1,0:T(8,128)S(1)}, f32[2048]{0:T(1024)S(1)}, s32[16,8]{1,0:T(8,128)S(1)}, bf16[64,16,128]{2,0,1:T(8,128)(2,1)S(1)}, /*in...) while((s32[]{:T(128)}, f32[8,128]{1,0:T(8,128)S(1)}, ...), condition=%wide.region_4.7_spmd, body=%wide.region_0.6_spmd.sunk | while | flops 17500104 | bytes 461323 | solution.py:63
  79.3 19.8 %psum.42 = f32[8,128]{1,0:T(8,128)S(1)} all-reduce(f32[8,128]{1,0:T(8,128)S(1)} %get-tuple-element.596), channel_id=1, replica_groups=mesh['imp'=8,'adv'=4] {'imp'}, use_global_device_ids=true, to_apply=%region_5.8 | all-reduce | flops 1024 | bytes 8192 | tf_op jit(solution)/shard_map/psum | solution.py:64
  99.7 16.1 %all-gather = f32[8,1,128]{2,1,0:T(1,128)S(1)} all-gather(f32[1,1,128]{2,1,0:T(1,128)S(1)} %bitcast.251), channel_id=1, replica_groups=mesh['imp'=8,'adv'=4] {'imp'}, dimensions={0}, use_global_device_ids=true | all-gather | bytes 4608 | tf_op jit(solution)/shard_map/all_gather | solution.py:44
  115.9 5.7 %psum.43 = f32[2048]{0:T(1024)S(1)} all-reduce(f32[2048]{0:T(1024)S(1)} %get-tuple-element.597), channel_id=1, replica_groups=mesh['imp'=8,'adv'=4] {'adv'}, use_global_device_ids=true, to_apply=%region_6.9 | all-reduce | flops 2048 | bytes 16384 | tf_op jit(solution)/shard_map/psum | solution.py:66
  122.3 42.2 %while.61 = (s32[]{:T(128)}, f32[8,128]{1,0:T(8,128)S(1)}, f32[2048]{0:T(1024)S(1)}, s32[16,8]{1,0:T(8,128)S(1)}, bf16[64,16,128]{2,0,1:T(8,128)(2,1)S(1)}, /*in...) while((s32[]{:T(128)}, f32[8,128]{1,0:T(8,128)S(1)}, ...), condition=%wide.region_11.14_spmd, body=%wide.region_7.13_spmd.sunk | while | flops 17631180 | bytes 458771 | solution.py:63
  164.6 19.1 %psum.44 = f32[8,128]{1,0:T(8,128)S(1)} all-reduce(f32[8,128]{1,0:T(8,128)S(1)} %get-tuple-element.598), channel_id=1, replica_groups=mesh['imp'=8,'adv'=4] {'imp'}, use_global_device_ids=true, to_apply=%region_12.15 | all-reduce | flops 1024 | bytes 8192 | tf_op jit(solution)/shard_map/psum | solution.py:64
  183.7 5.8 %psum.45 = f32[2048]{0:T(1024)S(1)} all-reduce(f32[2048]{0:T(1024)S(1)} %get-tuple-element.599), channel_id=1, replica_groups=mesh['imp'=8,'adv'=4] {'adv'}, use_global_device_ids=true, to_apply=%region_13.16 | all-reduce | flops 2048 | bytes 16384 | tf_op jit(solution)/shard_map/psum | solution.py:66
  189.5 42.2 %while.62 = (s32[]{:T(128)}, f32[8,128]{1,0:T(8,128)S(1)}, f32[2048]{0:T(1024)S(1)}, s32[16,8]{1,0:T(8,128)S(1)}, bf16[64,16,128]{2,0,1:T(8,128)(2,1)S(1)}, /*in...) while((s32[]{:T(128)}, f32[8,128]{1,0:T(8,128)S(1)}, ...), condition=%wide.region_18.21_spmd, body=%wide.region_14.20_spmd.sunk | while | flops 17631180 | bytes 458771 | solution.py:63
  231.8 6.9 %psum.47 = f32[2048]{0:T(1024)S(1)} all-reduce(f32[2048]{0:T(1024)S(1)} %get-tuple-element.601), channel_id=1, replica_groups=mesh['imp'=8,'adv'=4] {'adv'}, use_global_device_ids=true, to_apply=%region_20.23 | all-reduce | flops 2048 | bytes 16384 | tf_op jit(solution)/shard_map/psum | solution.py:66
  238.7 17.1 %psum.46 = f32[8,128]{1,0:T(8,128)S(1)} all-reduce(f32[8,128]{1,0:T(8,128)S(1)} %get-tuple-element.600), channel_id=1, replica_groups=mesh['imp'=8,'adv'=4] {'imp'}, use_global_device_ids=true, to_apply=%region_19.22 | all-reduce | flops 1024 | bytes 8192 | tf_op jit(solution)/shard_map/psum | solution.py:64
  255.9 51.6 %while.63 = (s32[]{:T(128)}, f32[64,2048]{1,0:T(8,128)S(1)}, f32[64,8,128]{2,0,1:T(8,128)S(1)}, s32[16,8]{1,0:T(8,128)S(1)}, bf16[64,8,128]{2,0,1:T(8,128)(2,1)S...) while((s32[]{:T(128)}, f32[64,2048]{1,0:T(8,128)S(1)}, ...), condition=%wide.region_23.26_spmd, body=%wide.region_21.25_spmd.sunk | while | flops 51185740 | bytes 2985015 | solution.py:91
  258.0 0.9 scatter_fusion
  261.2 0.9 scatter_fusion
  264.5 0.9 scatter_fusion
  267.7 0.9 scatter_fusion
  270.9 0.9 scatter_fusion
  274.1 0.9 scatter_fusion
  277.3 0.9 scatter_fusion
  280.6 0.9 scatter_fusion
  283.8 0.9 scatter_fusion
  287.0 0.9 scatter_fusion
  290.2 0.9 scatter_fusion
  293.5 0.9 scatter_fusion
  296.7 0.9 scatter_fusion
  299.9 0.9 scatter_fusion
  303.1 0.9 scatter_fusion
  310.3 58.0 %reduce-scatter.7.cloned.1.call-done = bf16[128,64]{1,0:T(8,128)(2,1)} async-done(((bf16[1024,64]{1,0:T(8,128)(2,1)}), bf16[128,64]{1,0:T(8,128)(2,1)}) %reduce-scatter.7.cloned.1.call-update) | async-done | bytes 16400
  368.4 1.4 copy.67
  369.8 21.8 %reduce-scatter.5.cloned.1.call-done = f32[64,512]{1,0:T(8,128)} async-done(((f32[64,2048]{1,0:T(8,128)}), f32[64,512]{1,0:T(8,128)}) %reduce-scatter.5.cloned.1.call-update) | async-done | bytes 131088 | tf_op jit(solution)/shard_map/reduce_scatter | solution.py:92
  391.6 1.5 convert_element_type.23
  (762 shorter events, 165.8 us)
Async XLA Ops:
  7.2 1.0 copy-start
  7.2 361.2 %reduce-scatter.7.cloned.1.call-start = ((), (), s32[]{:S(2)}) async-start(), calls=%async_computation.3 | async-start | bytes 294912
  8.1 0.7 copy-start.3
  36.7 0.7 copy-start.5
  37.5 0.7 copy-start.6
  99.1 0.7 copy-start.7
  121.6 0.7 copy-start.2
  307.5 0.6 copy-start.4
  307.5 1.5 copy-start.1
  309.0 82.6 %reduce-scatter.5.cloned.1.call-start = ((), (), s32[]{:S(2)}) async-start(), calls=%async_computation.2 | async-start | bytes 655360 | tf_op jit(solution)/shard_map/reduce_scatter | solution.py:92
Sparse Core Ops, SparseCore 0:
  309.1 59.2 reduce-scatter.6
  370.9 20.6 reduce-scatter.4
where the time goes:
time: 400 us
  blocking collectives  119 us (30%)
  local copies, waits for them, and re-layouts  99.7 us (25%)
  waiting for transfers between devices  80.5 us (20%)
  other arithmetic  51.6 us (13%)
  matrix products  30.9 us (8%)
  between operations  14.2 us (4%)
  loops' own time  4.38 us (1%)
    unnamed x3, waiting for transfers between devices  58.7 us
    psum x3, blocking collectives, local(): outlay = lax.psum(outlay, 'imp')  56.1 us
    gather x64, local copies, waits for them, and re-layouts, allocate(): columns = jnp.take(source, chosen, axis=1).reshape(features, extent)  36.6 us
    gather x64, local copies, waits for them, and re-layouts, allocate(): charged = jnp.take(prices, chosen, axis=0).reshape(extent)  35.6 us
    scatter-add x48, other arithmetic, advance(): outlay.at[chosen].add(jnp.sum(shares, axis=0).reshape(slot_count, BLOCK))  29 us
    all_gather x1, blocking collectives, local(): fetched = lax.all_gather(advertiser_vectors, 'imp', axis=1, tiled=True)  27.9 us
    dot_general x64, matrix products, allocate(): lax.dot_general(viewer, columns, (((0,), (0,)), ((), ())), preferred_elem...  23.6 us
    reduce_scatter x1, waiting for transfers between devices, local(): lax.psum_scatter(imp_part, 'adv', scatter_dimension=1, tiled=True)  21.8 us
  transfers between devices with their start and end apart: 2, of which 2 were waited for; matrix products, arithmetic and copies ran while one was open for 1% of the time, Pallas kernels for 0%

commit v1 on v0

v1 whole, which is shorter than its diff:
```python
import functools

import jax
import jax.numpy as jnp
from jax import lax
from jax.experimental import pallas as pl
from jax.experimental.pallas import tpu as pltpu
from jax.sharding import PartitionSpec as P

GROUP = 128
BLOCK = 128
ITERS = 3
FAR = 32768.0
ROWS = 16
MESH = pl.DeviceIdType.MESH
F32 = jnp.float32
BF16 = jnp.bfloat16


def pieces(x):
    a = x.astype(BF16).astype(F32)
    b = (x - a).astype(BF16).astype(F32)
    return a, b, x - a - b


def kernel(
    n_imp, n_adv, sizes,
    v_ref, a_ref, lim_ref, cap_ref, blk_ref, cnt_ref,
    prices_ref, duals_ref, ig_ref, ag_ref,
    vaug, aaug, at, cat, limb, lims, acc, outb, demb, pr, du, w,
    igs, igr, igown, ags, agr,
    g_send, g_recv, l_send, l_recv, o_send, o_recv, d_send, d_recv,
    i_send, i_recv, a_send, a_recv,
):
    feats, groups, slots, depth, wide, tall = sizes
    me_i, me_a = lax.axis_index("imp"), lax.axis_index("adv")
    imps = groups * GROUP
    advs = n_imp * BLOCK
    share = imps // n_adv

    def peer_i(s):
        return lax.rem(me_i + s, n_imp)

    def peer_a(s):
        return lax.rem(me_a + s, n_adv)

    def send(src, dst, ssem, rsem, device):
        return pltpu.make_async_remote_copy(
            src_ref=src, dst_ref=dst, send_sem=ssem, recv_sem=rsem, device_id=device, device_id_type=MESH
        )

    barrier = pltpu.get_barrier_semaphore()
    for s in range(1, n_imp):
        pl.semaphore_signal(barrier, inc=1, device_id={"imp": peer_i(s)}, device_id_type=MESH)
    for s in range(1, n_adv):
        pl.semaphore_signal(barrier, inc=1, device_id={"adv": peer_a(s)}, device_id_type=MESH)
    pl.semaphore_wait(barrier, n_imp + n_adv - 2)

    def gather_copies(s):
        there = {"imp": peer_i(s)}
        return (
            send(a_ref, cat.at[me_i], g_send.at[s], g_recv.at[s], there),
            send(lim_ref, limb.at[me_i], l_send.at[s], l_recv.at[s], there),
        )

    for s in range(1, n_imp):
        for copy in gather_copies(s):
            copy.start()

    head = feats
    mask_at = feats + ROWS
    cat[me_i] = a_ref[...]
    limb[me_i] = lim_ref[...]
    vaug[0:feats, :] = v_ref[...]
    vaug[mask_at:depth, :] = jnp.where(
        lax.broadcasted_iota(jnp.int32, (depth - mask_at, imps), 0)
        == lax.broadcasted_iota(jnp.int32, (depth - mask_at, imps), 1) // GROUP,
        1.0, 0.0,
    ).astype(BF16)
    served = lax.broadcasted_iota(jnp.int32, (groups, advs), 1) // BLOCK * n_adv + me_a
    barred = jnp.full((groups, advs), -FAR, F32)
    counts = cnt_ref[...]
    for k in range(slots):
        named = jnp.where(counts > k, blk_ref[:, k : k + 1], -1)
        barred = jnp.where(named == served, 0.0, barred)
    aaug[mask_at : mask_at + groups, :] = barred.astype(BF16)
    if depth > mask_at + groups:
        aaug[mask_at + groups : depth, :] = jnp.zeros((depth - mask_at - groups, advs), BF16)

    row = lax.broadcasted_iota(jnp.int32, (ROWS, 128), 0)

    def put(ref, values, count, sign, first, ones):
        fixed = jnp.where((row >= ones) & (row < ones + 3), sign, 0.0)
        a, b, c = pieces(values * sign)
        for i in range(count):
            tile = jnp.where(row == first, a[i : i + 1, :], fixed)
            tile = jnp.where(row == first + 1, b[i : i + 1, :], tile)
            tile = jnp.where(row == first + 2, c[i : i + 1, :], tile)
            ref[head : head + ROWS, i * 128 : (i + 1) * 128] = tile.astype(BF16)

    pr[...] = jnp.zeros_like(pr)
    du[...] = jnp.zeros_like(du)
    put(vaug, du[...], groups, 1.0, 0, 3)

    def set_prices():
        put(aaug, pr[...], n_imp, -1.0, 3, 0)
        at[...] = aaug[...].T

    for s in range(1, n_imp):
        for copy in gather_copies(s):
            copy.wait_recv()
    for b in range(n_imp):
        aaug[0:feats, b * BLOCK : (b + 1) * BLOCK] = cat[b]
        lims[b : b + 1, :] = limb[b]
    set_prices()

    def tile_shares(rows, columns):
        scores = jnp.dot(at[rows, :], vaug[:, columns], preferred_element_type=F32)
        return jnp.minimum(jnp.maximum(scores, 0.0), 1.0)

    for it in range(ITERS):
        acc[...] = jnp.zeros_like(acc)

        def advance(c, carry):
            columns = pl.ds(pl.multiple_of(c * wide, wide), wide)
            demand = jnp.zeros((1, wide), F32)
            for t in range(advs // tall):
                rows = slice(t * tall, (t + 1) * tall)
                shares = tile_shares(rows, columns)
                demand = demand + jnp.sum(shares, axis=0, keepdims=True)
                total = shares[:, 0:GROUP]
                for h in range(1, wide // GROUP):
                    total = total + shares[:, h * GROUP : (h + 1) * GROUP]
                acc[rows, :] += total
            for h in range(wide // GROUP):
                demb[it, me_a, pl.ds(c * (wide // GROUP) + h, 1), :] = demand[:, h * GROUP : (h + 1) * GROUP]
            return carry

        lax.fori_loop(0, imps // wide, advance, 0)

        def demand_copy(s):
            slot = demb.at[it, me_a]
            return send(slot, slot, d_send.at[it, s], d_recv.at[it, s], {"adv": peer_a(s)})

        def outlay_copy(s):
            slot = outb.at[it, me_i]
            return send(slot, slot, o_send.at[it, s], o_recv.at[it, s], {"imp": peer_i(s)})

        for s in range(1, n_adv):
            demand_copy(s).start()
        for b in range(n_imp):
            outb[it, me_i, b : b + 1, :] = jnp.sum(
                acc[b * BLOCK : (b + 1) * BLOCK, :].T, axis=0, keepdims=True
            )
        for s in range(1, n_imp):
            outlay_copy(s).start()
        for s in range(1, n_adv):
            demand_copy(s).wait_recv()
        demand = demb[it, 0]
        for a in range(1, n_adv):
            demand = demand + demb[it, a]
        du[...] = jnp.maximum(du[...] + demand / cap_ref[...] - 1.0, 0.0)
        put(vaug, du[...], groups, 1.0, 0, 3)
        for s in range(1, n_imp):
            outlay_copy(s).wait_recv()
        outlay = outb[it, 0]
        for b in range(1, n_imp):
            outlay = outlay + outb[it, b]
        pr[...] = jnp.maximum(pr[...] + outlay / lims[...] - 1.0, 0.0)
        set_prices()

    def imp_terms(s, c):
        base = peer_a(s) * share + c * wide
        columns = pl.ds(pl.multiple_of(base, wide), wide)
        total = jnp.zeros((feats, wide), F32)
        for t in range(advs // tall):
            rows = slice(t * tall, (t + 1) * tall)
            weights = tile_shares(rows, columns).astype(BF16)
            w[rows, columns] = weights
            total = total + jnp.dot(aaug[0:feats, rows], weights, preferred_element_type=F32)
        return total

    def imp_copy(s):
        return send(igs.at[s], igr.at[s], i_send.at[s], i_recv.at[s], {"adv": peer_a(s)})

    def imp_step(s, carry):
        for c in range(share // wide):
            igs[s, :, c * wide : (c + 1) * wide] = imp_terms(s, c).astype(BF16)
        imp_copy(s).start()
        return carry

    lax.fori_loop(1, n_adv, imp_step, 0)
    for c in range(share // wide):
        igown[:, c * wide : (c + 1) * wide] = imp_terms(0, c)

    def adv_terms(s):
        rows = pl.ds(pl.multiple_of(peer_i(s) * BLOCK, BLOCK), BLOCK)
        terms = lax.dot_general(
            vaug[0:feats, :], w[rows, :], (((1,), (1,)), ((), ())), preferred_element_type=F32
        )
        return (terms * (1.0 / GROUP)).astype(BF16)

    def adv_copy(s):
        return send(ags.at[s], agr.at[s], a_send.at[s], a_recv.at[s], {"imp": peer_i(s)})

    def adv_step(s, carry):
        ags[s] = adv_terms(s)
        adv_copy(s).start()
        return carry

    lax.fori_loop(1, n_imp, adv_step, 0)
    own = adv_terms(0).astype(F32)
    prices_ref[...] = pr[pl.ds(me_i, 1), :]
    duals_ref[...] = du[...]
    for s in range(1, n_adv):
        imp_copy(s).wait_recv()
    total = igown[...]
    for s in range(1, n_adv):
        total = total + igr[s].astype(F32)
    ig_ref[...] = total.astype(BF16)
    for s in range(1, n_imp):
        adv_copy(s).wait_recv()
        own = own + agr[s].astype(F32)
    ag_ref[...] = own.astype(BF16)

    for s in range(1, n_imp):
        for copy in gather_copies(s):
            copy.wait_send()
        for it in range(ITERS):
            slot = outb.at[it, me_i]
            send(slot, slot, o_send.at[it, s], o_recv.at[it, s], {"imp": peer_i(s)}).wait_send()
        adv_copy(s).wait_send()
    for s in range(1, n_adv):
        for it in range(ITERS):
            slot = demb.at[it, me_a]
            send(slot, slot, d_send.at[it, s], d_recv.at[it, s], {"adv": peer_a(s)}).wait_send()
        imp_copy(s).wait_send()


def local(impression_vectors, advertiser_vectors, spend_limits, capacity, blocks, counts):
    feats, imps = impression_vectors.shape
    groups, _, slots = blocks.shape
    n_imp, n_adv = lax.axis_size("imp"), lax.axis_size("adv")
    advs = n_imp * BLOCK
    depth = -(-(feats + ROWS + groups) // 128) * 128
    share = imps // n_adv
    wide = min(256, share)
    tall = min(1024, advs)
    dma = pltpu.SemaphoreType.DMA
    vmem = pl.BlockSpec(memory_space=pltpu.VMEM)
    prices, duals, imp_grad, adv_grad = pl.pallas_call(
        functools.partial(kernel, n_imp, n_adv, (feats, groups, slots, depth, wide, tall)),
        out_shape=(
            jax.ShapeDtypeStruct((1, BLOCK), F32),
            jax.ShapeDtypeStruct((groups, GROUP), F32),
            jax.ShapeDtypeStruct((feats, share), BF16),
            jax.ShapeDtypeStruct((feats, BLOCK), BF16),
        ),
        in_specs=[vmem] * 6,
        out_specs=(vmem,) * 4,
        scratch_shapes=[
            pltpu.VMEM((depth, imps), BF16),
            pltpu.VMEM((depth, advs), BF16),
            pltpu.VMEM((advs, depth), BF16),
            pltpu.VMEM((n_imp, feats, BLOCK), BF16),
            pltpu.VMEM((n_imp, 1, BLOCK), F32),
            pltpu.VMEM((n_imp, BLOCK), F32),
            pltpu.VMEM((advs, GROUP), F32),
            pltpu.VMEM((ITERS, n_imp, n_imp, BLOCK), F32),
            pltpu.VMEM((ITERS, n_adv, groups, GROUP), F32),
            pltpu.VMEM((n_imp, BLOCK), F32),
            pltpu.VMEM((groups, GROUP), F32),
            pltpu.VMEM((advs, imps), BF16),
            pltpu.VMEM((n_adv, feats, share), BF16),
            pltpu.VMEM((n_adv, feats, share), BF16),
            pltpu.VMEM((feats, share), F32),
            pltpu.VMEM((n_imp, feats, BLOCK), BF16),
            pltpu.VMEM((n_imp, feats, BLOCK), BF16),
            dma((n_imp,)), dma((n_imp,)), dma((n_imp,)), dma((n_imp,)),
            dma((ITERS, n_imp)), dma((ITERS, n_imp)), dma((ITERS, n_adv)), dma((ITERS, n_adv)),
            dma((n_adv,)), dma((n_adv,)), dma((n_imp,)), dma((n_imp,)),
        ],
        compiler_params=pltpu.CompilerParams(
            collective_id=0, has_side_effects=True, vmem_limit_bytes=48 * 1024 * 1024
        ),
    )(
        impression_vectors,
        advertiser_vectors,
        spend_limits.reshape(1, BLOCK),
        capacity.reshape(groups, GROUP),
        blocks.reshape(groups, slots),
        counts,
    )
    return prices.reshape(-1), duals.reshape(-1), imp_grad, adv_grad


def solution(mesh):
    return jax.shard_map(
        local,
        mesh=mesh,
        in_specs=(
            P(None, "imp"),
            P(None, ("imp", "adv")),
            P(("imp", "adv")),
            P("imp"),
            P("imp", "adv", None),
            P("imp", "adv"),
        ),
        out_specs=(P(("imp", "adv")), P("imp"), P(None, ("imp", "adv")), P(None, ("imp", "adv"))),
        check_vma=False,
    )
```

time: 400 us -> 48.6 us (0.12)
  blocking collectives: 119 us -> 0 us
  local copies, waits for them, and re-layouts: 99.7 us -> 4.72 us
  waiting for transfers between devices: 80.5 us -> 0 us
  other arithmetic: 51.6 us -> 0 us
  Pallas kernels: 0 us -> 43 us
  matrix products: 30.9 us -> 0 us
  between operations: 14.2 us -> 0.67 us
  loops' own time: 4.38 us -> 0 us
    psum x6 -> x0, blocking collectives: 74.5 us -> none  [the longest x3 56.1 us: local(): outlay = lax.psum(outlay, 'imp')]
    gather x128 -> x0, local copies, waits for them, and re-layouts: 72.2 us -> none  [the longest x64 36.6 us: allocate(): columns = jnp.take(source, chosen, axis=1).reshape(features, extent)]
    unnamed x3 -> x0, waiting for transfers between devices: 58.7 us -> none
    all_gather x2 -> x0, blocking collectives: 44 us -> none  [the longest x1 27.9 us: local(): fetched = lax.all_gather(advertiser_vectors, 'imp', axis=1, tiled=True)]
    scatter-add x64 -> x0, other arithmetic: 43.2 us -> none  [the longest x48 29 us: advance(): outlay.at[chosen].add(jnp.sum(shares, axis=0).reshape(slot_count, BLOCK))]
    pallas_call x0 -> x1, Pallas kernels: none -> 43 us  [local(): pl.pallas_call(functools.partial(kernel, n_imp, n_adv, (feats, groups, sl...]
    dot_general x96 -> x0, matrix products: 30.9 us -> none  [the longest x64 23.6 us: allocate(): lax.dot_general(viewer, columns, (((0,), (0,)), ((), ())), preferred_elem...]
    reduce_scatter x1 -> x0, waiting for transfers between devices: 21.8 us -> none  [local(): lax.psum_scatter(imp_part, 'adv', scatter_dimension=1, tiled=True)]
  transfers between devices with their start and end apart: 2 -> 0, of which waited for: 2 -> 0; matrix products, arithmetic and copies ran while one was open for 1% -> 0% of each run, Pallas kernels for 0% -> 0%
where the time goes in v1:
time: 48.6 us; the launch traced here: 48.4 us
  Pallas kernels  43 us (88%)
  local copies, waits for them, and re-layouts  4.72 us (10%)
  between operations  0.67 us (1%)
    pallas_call x1, Pallas kernels, local(): pl.pallas_call(functools.partial(kernel, n_imp, n_adv, (feats, groups, sl...  43 us
    unnamed x15, local copies, waits for them, and re-layouts  3.96 us

profile of v1, /device:TPU:0, one launch (start us, length us, event | category | flops | bytes accessed | tf_op | source)
XLA Modules:
  0.0 48.4 jit_solution(7624719143321942794)
XLA Ops:
  0.6 0.0 copy-start.1
  0.6 0.0 copy-start.4
  0.7 0.0 copy-start.2
  0.7 0.8 %copy.10.blk_ref = s32[16,8]{1,0:T(8,128)S(1)} copy(s32[16,8]{0,1:T(8,128)} %bitcast.9) | data formatting | bytes 1024 | tf_op jit(solution)/shard_map/reshape | solution.py:291
  1.4 0.0 copy-done.4
  1.4 0.0 copy-start.3
  1.4 0.1 copy.11.cnt_ref
  1.5 0.0 copy-done.1
  1.5 0.0 copy-done.2
  1.5 0.6 %copy-done.3 = f32[128]{0:T(128)S(1)} copy-done((f32[128]{0:T(128)S(1)}, f32[128]{0:T(128)}, u32[]{:S(2)}) %copy-start.3) | copy-done | bytes 536
  2.1 0.0 copy-start
  2.1 0.9 %copy-done = bf16[64,2048]{1,0:T(8,128)(2,1)S(1)} copy-done((bf16[64,2048]{1,0:T(8,128)(2,1)S(1)}, bf16[64,2048]{1,0:T(8,128)(2,1)}, u32[]{:S(2)}) %copy-start) | copy-done | bytes 262168
  3.0 43.0 %shard_map.93 = (f32[1,128]{1,0:T(1,128)S(1)}, f32[16,128]{1,0:T(8,128)S(1)}, bf16[64,512]{1,0:T(8,128)(2,1)S(1)}, bf16[64,128]{1,0:T(8,128)(2,1)S(1)}) custom-call(bf16[64,2048]{1,0:T(8,128)(2,1)S(1)} %copy-done, bf16[64,128]{1,0:T(8,128)(2,1)S(1)} %copy-done.1, f32[1,128]{1,0:T(1,128)S(1)} %bitcast.7, f32[16,128]{1,0:T(8,128)S(1)} %bitcast.5, ...), custom_call_target="tpu_custom_call" | custom-call | tf_op jit(solution)/shard_map/pallas_call | solution.py:251
  46.0 0.5 %copy.16 = f32[128]{0:T(128)} copy(f32[128]{0:T(128)S(1)} %bitcast.8) | data formatting | bytes 1024
  46.6 0.6 %copy.17 = f32[2048]{0:T(1024)} copy(f32[2048]{0:T(1024)S(1)} %bitcast.6) | data formatting | bytes 16384
  47.2 0.6 %copy.18 = bf16[64,512]{1,0:T(8,128)(2,1)} copy(bf16[64,512]{1,0:T(8,128)(2,1)S(1)} %get-tuple-element.18) | data formatting | bytes 131072
  47.8 0.6 %copy.19 = bf16[64,128]{1,0:T(8,128)(2,1)} copy(bf16[64,128]{1,0:T(8,128)(2,1)S(1)} %get-tuple-element.19) | data formatting | bytes 32768
Async XLA Ops:
  0.6 0.9 %copy-start.1 = (bf16[64,128]{1,0:T(8,128)(2,1)S(1)}, bf16[64,128]{1,0:T(8,128)(2,1)}, u32[]{:S(2)}) copy-start(bf16[64,128]{1,0:T(8,128)(2,1)} %a_ref.1) | copy-start | bytes 49156
  0.6 0.8 %copy-start.4 = (s32[16,1]{0,1:T(1,128)S(1)}, s32[16,1]{0,1:T(1,128)}, u32[]{:S(2)}) copy-start(s32[16,1]{0,1:T(1,128)} %param.11) | copy-start | bytes 196
  0.7 0.9 %copy-start.2 = (f32[2048]{0:T(1024)S(1)}, f32[2048]{0:T(1024)}, u32[]{:S(2)}) copy-start(f32[2048]{0:T(1024)} %param.9) | copy-start | bytes 24580
  1.4 0.7 %copy-start.3 = (f32[128]{0:T(128)S(1)}, f32[128]{0:T(128)}, u32[]{:S(2)}) copy-start(f32[128]{0:T(128)} %param.8) | copy-start | bytes 1540
  2.1 0.9 %copy-start = (bf16[64,2048]{1,0:T(8,128)(2,1)S(1)}, bf16[64,2048]{1,0:T(8,128)(2,1)}, u32[]{:S(2)}) copy-start(bf16[64,2048]{1,0:T(8,128)(2,1)} %v_ref.1) | copy-start | bytes 786436
